TPU v7x, 512 devices: a whole 4x8x8 slice. The times are simulated.
512 devices in a mesh: energy: 64 (over x, y_hi, z), slab: 8 (over y_lo, core).
Axes of the slice: x: 4, y: 8 (y_hi: 2, y_lo: 4; y = y_hi * 4 + y_lo), z: 8, core: 2. Of those that a mesh axis runs over, the one named last changes fastest.
Arguments:
- green0: bfloat16 [64, 8, 2, 384, 384], P('energy', 'slab'), may hold values from -6 to 6
- coupling: bfloat16 [8, 3, 384, 384], P('slab'), may hold values from -0.09375 to 0.09375
Outputs:
- green: bfloat16 [64, 8, 2, 384, 384], P('energy', 'slab')
All inputs are finite; a program needn't handle non-finite values.
Results may differ from a plain program's by a relative error of at most 0.012.
Values may be sent and summed in bfloat16 or wider, within the bound.
A program may use at most 64 MiB of HBM per device.

v0:
```python
import jax
import jax.numpy as jnp
from jax import lax
from jax.sharding import PartitionSpec as P

OFFSET = 7
ITERS = 2


def passed_along(value, axis, steps):
    count = lax.axis_size(axis)
    first, last = (max(0, -steps), min(count, count - steps))
    return lax.ppermute(value, axis, [(source, source + steps) for source in range(first, last)])


def with_halo(block, sides, width):
    for axis, dim in sides:
        count = lax.axis_size(axis)
        forward = [(i, i + 1) for i in range(count - 1)]
        backward = [(target, source) for source, target in forward]
        low = lax.ppermute(
            lax.slice_in_dim(block, block.shape[dim] - width, None, axis=dim), axis, forward
        )
        high = lax.ppermute(lax.slice_in_dim(block, 0, width, axis=dim), axis, backward)
        block = jnp.concatenate([low, block, high], axis=dim)
    return block


def dyson(green0, coupling, summed):
    count = green0.shape[1]
    size = green0.shape[-1]
    sigma = jnp.zeros(green0.shape, jnp.float32)
    for index in range(3):
        part = summed[:, index : index + count]
        weights = coupling[:, index]
        left = jnp.einsum(
            "sij,escjk->escik", weights, part, preferred_element_type=jnp.float32
        ).astype(jnp.bfloat16)
        sigma = sigma + jnp.einsum(
            "escij,skj->escik", left, weights, preferred_element_type=jnp.float32
        )
    sigma = sigma.astype(jnp.bfloat16)
    green_re = green0[:, :, 0]
    green_im = green0[:, :, 1]
    form = "esij,esjk->esik"
    prod_re = jnp.einsum(
        form, green_re, sigma[:, :, 0], preferred_element_type=jnp.float32
    ) - jnp.einsum(form, green_im, sigma[:, :, 1], preferred_element_type=jnp.float32)
    prod_im = jnp.einsum(
        form, green_re, sigma[:, :, 1], preferred_element_type=jnp.float32
    ) + jnp.einsum(form, green_im, sigma[:, :, 0], preferred_element_type=jnp.float32)
    prod_re = prod_re.astype(jnp.bfloat16)
    prod_im = prod_im.astype(jnp.bfloat16)
    trans = "esij,eskj->esik"
    out_re = jnp.einsum(trans, prod_re, green_re, preferred_element_type=jnp.float32) - jnp.einsum(
        trans, prod_im, green_im, preferred_element_type=jnp.float32
    )
    out_im = jnp.einsum(trans, prod_re, green_im, preferred_element_type=jnp.float32) + jnp.einsum(
        trans, prod_im, green_re, preferred_element_type=jnp.float32
    )
    result = green0.astype(jnp.float32) + jnp.stack([out_re, out_im], axis=2) / size
    return result.astype(jnp.bfloat16)


def local(green0, coupling):
    green = green0
    for turn in range(ITERS):
        lower = passed_along(green, "energy", OFFSET)
        upper = passed_along(green, "energy", -OFFSET)
        own_sum = (lower.astype(jnp.float32) + upper.astype(jnp.float32)).astype(jnp.bfloat16)
        summed = with_halo(own_sum, (("slab", 1),), 1)
        green = dyson(green0, coupling, summed)
    return green


def solution(mesh):
    placed = (P("energy", "slab", None, None, None), P("slab", None, None, None))
    return jax.shard_map(
        local,
        mesh=mesh,
        in_specs=placed,
        out_specs=P("energy", "slab", None, None, None),
        check_vma=False,
    )
```

profile of v0, /device:TPU:468, one launch (start us, length us, event | category | flops | bytes accessed | tf_op | source)
XLA Modules:
  0.0 166.8 jit_solution(13789588275280365018)
XLA Ops:
  0.0 1.4 copy.3
  1.5 5.9 %collective-permute-start = (bf16[1,1,2,384,384]{3,4,2,1,0:T(8,128)(2,1)S(1)}, bf16[1,1,2,384,384]{3,4,2,1,0:T(8,128)(2,1)S(1)}, u32[]{:S(2)}, u32[]{:S(2)}) collective-permute-start(bf16[1,1,2,384,384]{3,4,2,1,0:T(8,128)(2,1)S(1)} %copy.3), channel_id=1, source_target_pairs={{0,56},{8,64},{16,72},{24,80},{32,88},{40,96},{48,104},{56,112},{6... | collective-permute-start | bytes 1769480 | tf_op jit(solution)/shard_map/ppermute | solution.py:13
  7.4 1.9 %collective-permute-start.1 = (bf16[1,1,2,384,384]{3,4,2,1,0:T(8,128)(2,1)S(1)}, bf16[1,1,2,384,384]{3,4,2,1,0:T(8,128)(2,1)S(1)}, u32[]{:S(2)}, u32[]{:S(2)}) collective-permute-start(bf16[1,1,2,384,384]{3,4,2,1,0:T(8,128)(2,1)S(1)} %copy.3), channel_id=1, source_target_pairs={{56,0},{64,8},{72,16},{80,24},{88,32},{96,40},{104,48},{112,56},{1... | collective-permute-start | bytes 1769480 | tf_op jit(solution)/shard_map/ppermute | solution.py:13
  9.3 23.3 %collective-permute-done = bf16[1,1,2,384,384]{3,4,2,1,0:T(8,128)(2,1)S(1)} collective-permute-done((bf16[1,1,2,384,384]{3,4,2,1,0:T(8,128)(2,1)S(1)}, bf16[1,1,2,384,384]{3,4,2,1,0:T(8,128)(2,1)S(1)}, u32[]{:S(2)}, u32[]{:S(2)}) %collective-permute-start) | collective-permute-done | bytes 589856 | tf_op jit(solution)/shard_map/ppermute | solution.py:13
  32.6 28.1 %collective-permute-done.1 = bf16[1,1,2,384,384]{3,4,2,1,0:T(8,128)(2,1)S(1)} collective-permute-done((bf16[1,1,2,384,384]{3,4,2,1,0:T(8,128)(2,1)S(1)}, bf16[1,1,2,384,384]{3,4,2,1,0:T(8,128)(2,1)S(1)}, u32[]{:S(2)}, u32[]{:S(2)}) %collective-permute-start.1) | collective-permute-done | bytes 589856 | tf_op jit(solution)/shard_map/ppermute | solution.py:13
  60.8 1.9 %collective-permute-start.2 = (bf16[1,1,2,384,384]{3,4,2,1,0:T(8,128)(2,1)S(1)}, bf16[1,1,2,384,384]{3,4,2,1,0:T(8,128)(2,1)S(1)}, u32[]{:S(2)}, u32[]{:S(2)}) collective-permute-start(bf16[1,1,2,384,384]{3,4,2,1,0:T(8,128)(2,1)S(1)} %add_convert_fusion.1), channel_id=1, source_target_pairs={{0,1},{1,2},{2,3},{3,4},{4,5},{5,6},{6,7},{8,9},{9,10},{10,11},{11... | collective-permute-start | bytes 1769480 | tf_op jit(solution)/shard_map/ppermute | solution.py:21
  62.8 3.6 %collective-permute-start.3 = (bf16[1,1,2,384,384]{3,4,2,1,0:T(8,128)(2,1)S(1)}, bf16[1,1,2,384,384]{3,4,2,1,0:T(8,128)(2,1)}, u32[]{:S(2)}, u32[]{:S(2)}) collective-permute-start(bf16[1,1,2,384,384]{3,4,2,1,0:T(8,128)(2,1)S(1)} %add_convert_fusion.1), channel_id=1, source_target_pairs={{1,0},{2,1},{3,2},{4,3},{5,4},{6,5},{7,6},{9,8},{10,9},{11,10},{12... | collective-permute-start | bytes 1769480 | tf_op jit(solution)/shard_map/ppermute | solution.py:24
  66.4 5.6 %collective-permute-done.2 = bf16[1,1,2,384,384]{3,4,2,1,0:T(8,128)(2,1)S(1)} collective-permute-done((bf16[1,1,2,384,384]{3,4,2,1,0:T(8,128)(2,1)S(1)}, bf16[1,1,2,384,384]{3,4,2,1,0:T(8,128)(2,1)S(1)}, u32[]{:S(2)}, u32[]{:S(2)}) %collective-permute-start.2) | collective-permute-done | bytes 589856 | tf_op jit(solution)/shard_map/ppermute | solution.py:21
  72.0 1.0 fusion.9
  73.1 2.1 %convolution_add_fusion.3 = f32[2,384,384]{2,1,0:T(8,128)} fusion(f32[2,384,384]{2,1,0:T(8,128)S(1)} %fusion.9, bf16[1,1,2,384,384]{3,4,2,1,0:T(8,128)(2,1)S(1)} %add_convert_fusion.1, bf16[1,3,384,384]{3,2,1,0:T(8,128)(2,1)S(1)} %copy-done.1), kind=kOutput, calls=%fused_computation.5 | convolution fusion | flops 453574656 | bytes 3538944 | tf_op jit(solution)/shard_map/escij,skj->escik/dot_general | solution.py:39
  75.1 2.5 %fusion.3 = bf16[1,1,2,384,384]{4,3,2,0,1:T(8,128)(2,1)S(1)} fusion(f32[2,384,384]{2,1,0:T(8,128)} %convolution_add_fusion.3, bf16[1,1,2,384,384]{3,4,2,1,0:T(8,128)(2,1)} %collective-permute-done.3, bf16[1,3,384,384]{3,2,1,0:T(8,128)(2,1)S(1)} %copy-done.1), kind=kOutput, calls=%fused_computation.15 | convolution fusion | flops 453869568 | bytes 2949120 | tf_op jit(solution)/shard_map/escij,skj->escik/dot_general | solution.py:39
  78.1 0.4 fusion.68
  78.5 0.4 fusion.16
  78.9 0.4 fusion.66
  79.3 0.4 fusion.51
  79.7 0.4 fusion.17
  80.2 0.4 fusion.7
  80.6 0.4 fusion.6
  81.2 30.3 %collective-permute-start.4 = (bf16[1,1,2,384,384]{4,3,2,1,0:T(8,128)(2,1)S(1)}, bf16[1,1,2,384,384]{4,3,2,1,0:T(8,128)(2,1)S(1)}, u32[]{:S(2)}, u32[]{:S(2)}) collective-permute-start(bf16[1,1,2,384,384]{4,3,2,1,0:T(8,128)(2,1)S(1)} %fusion.20), channel_id=1, source_target_pairs={{0,56},{8,64},{16,72},{24,80},{32,88},{40,96},{48,104},{56,112},{6... | collective-permute-start | bytes 1769480 | tf_op jit(solution)/shard_map/ppermute | solution.py:13
  111.4 1.9 %collective-permute-start.5 = (bf16[1,1,2,384,384]{4,3,2,1,0:T(8,128)(2,1)S(1)}, bf16[1,1,2,384,384]{4,3,2,1,0:T(8,128)(2,1)S(1)}, u32[]{:S(2)}, u32[]{:S(2)}) collective-permute-start(bf16[1,1,2,384,384]{4,3,2,1,0:T(8,128)(2,1)S(1)} %fusion.20), channel_id=1, source_target_pairs={{56,0},{64,8},{72,16},{80,24},{88,32},{96,40},{104,48},{112,56},{1... | collective-permute-start | bytes 1769480 | tf_op jit(solution)/shard_map/ppermute | solution.py:13
  113.4 17.7 %collective-permute-done.4 = bf16[1,1,2,384,384]{4,3,2,1,0:T(8,128)(2,1)S(1)} collective-permute-done((bf16[1,1,2,384,384]{4,3,2,1,0:T(8,128)(2,1)S(1)}, bf16[1,1,2,384,384]{4,3,2,1,0:T(8,128)(2,1)S(1)}, u32[]{:S(2)}, u32[]{:S(2)}) %collective-permute-start.4) | collective-permute-done | bytes 589856 | tf_op jit(solution)/shard_map/ppermute | solution.py:13
  131.1 13.3 %collective-permute-done.5 = bf16[1,1,2,384,384]{4,3,2,1,0:T(8,128)(2,1)S(1)} collective-permute-done((bf16[1,1,2,384,384]{4,3,2,1,0:T(8,128)(2,1)S(1)}, bf16[1,1,2,384,384]{4,3,2,1,0:T(8,128)(2,1)S(1)}, u32[]{:S(2)}, u32[]{:S(2)}) %collective-permute-start.5) | collective-permute-done | bytes 589856 | tf_op jit(solution)/shard_map/ppermute | solution.py:13
  144.6 1.9 %collective-permute-start.6 = (bf16[1,1,2,384,384]{4,3,2,1,0:T(8,128)(2,1)S(1)}, bf16[1,1,2,384,384]{4,3,2,1,0:T(8,128)(2,1)}, u32[]{:S(2)}, u32[]{:S(2)}) collective-permute-start(bf16[1,1,2,384,384]{4,3,2,1,0:T(8,128)(2,1)S(1)} %add_convert_fusion), channel_id=1, source_target_pairs={{0,1},{1,2},{2,3},{3,4},{4,5},{5,6},{6,7},{8,9},{9,10},{10,11},{11... | collective-permute-start | bytes 1769480 | tf_op jit(solution)/shard_map/ppermute | solution.py:21
  146.5 3.8 %collective-permute-start.7 = (bf16[1,1,2,384,384]{4,3,2,1,0:T(8,128)(2,1)S(1)}, bf16[1,1,2,384,384]{4,3,2,1,0:T(8,128)(2,1)}, u32[]{:S(2)}, u32[]{:S(2)}) collective-permute-start(bf16[1,1,2,384,384]{4,3,2,1,0:T(8,128)(2,1)S(1)} %add_convert_fusion), channel_id=1, source_target_pairs={{1,0},{2,1},{3,2},{4,3},{5,4},{6,5},{7,6},{9,8},{10,9},{11,10},{12... | collective-permute-start | bytes 1769480 | tf_op jit(solution)/shard_map/ppermute | solution.py:24
  150.3 5.5 %collective-permute-done.6 = bf16[1,1,2,384,384]{4,3,2,1,0:T(8,128)(2,1)} collective-permute-done((bf16[1,1,2,384,384]{4,3,2,1,0:T(8,128)(2,1)S(1)}, bf16[1,1,2,384,384]{4,3,2,1,0:T(8,128)(2,1)}, u32[]{:S(2)}, u32[]{:S(2)}) %collective-permute-start.6) | collective-permute-done | bytes 589856 | tf_op jit(solution)/shard_map/ppermute | solution.py:21
  155.9 2.1 %fusion.13 = f32[2,384,384]{2,1,0:T(8,128)S(1)} fusion(bf16[1,1,2,384,384]{4,3,2,1,0:T(8,128)(2,1)} %collective-permute-done.6, bf16[1,3,384,384]{3,2,1,0:T(8,128)(2,1)S(1)} %copy-done.1), kind=kOutput, calls=%fused_computation.33 | convolution fusion | flops 453279744 | bytes 2359296 | tf_op jit(solution)/shard_map/escij,skj->escik/dot_general | solution.py:39
  158.0 2.1 %convolution_add_fusion.1 = f32[2,384,384]{2,1,0:T(8,128)} fusion(f32[2,384,384]{2,1,0:T(8,128)S(1)} %fusion.13, bf16[1,1,2,384,384]{4,3,2,1,0:T(8,128)(2,1)S(1)} %add_convert_fusion, bf16[1,3,384,384]{3,2,1,0:T(8,128)(2,1)S(1)} %copy-done.1), kind=kOutput, calls=%fused_computation.3 | convolution fusion | flops 453574656 | bytes 3538944 | tf_op jit(solution)/shard_map/escij,skj->escik/dot_general | solution.py:39
  160.1 2.5 %fusion.2 = bf16[1,1,2,384,384]{4,3,2,0,1:T(8,128)(2,1)S(1)} fusion(f32[2,384,384]{2,1,0:T(8,128)} %convolution_add_fusion.1, bf16[1,1,2,384,384]{4,3,2,1,0:T(8,128)(2,1)} %collective-permute-done.7, bf16[1,3,384,384]{3,2,1,0:T(8,128)(2,1)S(1)} %copy-done.1), kind=kOutput, calls=%fused_computation.14 | convolution fusion | flops 453869568 | bytes 2949120 | tf_op jit(solution)/shard_map/escij,skj->escik/dot_general | solution.py:39
  163.4 0.4 fusion.18
  164.6 0.4 fusion.19
  165.0 0.4 fusion.5
  165.9 1.0 fusion.21
  (15 shorter events, 2.9 us)
Async XLA Ops:
  0.0 72.0 %copy-start.1 = (bf16[1,3,384,384]{3,2,1,0:T(8,128)(2,1)S(1)}, bf16[1,3,384,384]{3,2,1,0:T(8,128)(2,1)}, u32[]{:S(2)}) copy-start(bf16[1,3,384,384]{3,2,1,0:T(8,128)(2,1)} %param.3) | copy-start | bytes 2654212
  1.5 31.1 %collective-permute-start = (bf16[1,1,2,384,384]{3,4,2,1,0:T(8,128)(2,1)S(1)}, bf16[1,1,2,384,384]{3,4,2,1,0:T(8,128)(2,1)S(1)}, u32[]{:S(2)}, u32[]{:S(2)}) collective-permute-start(bf16[1,1,2,384,384]{3,4,2,1,0:T(8,128)(2,1)S(1)} %copy.3), channel_id=1, source_target_pairs={{0,56},{8,64},{16,72},{24,80},{32,88},{40,96},{48,104},{56,112},{6... | collective-permute-start | bytes 1769480 | tf_op jit(solution)/shard_map/ppermute | solution.py:13
  7.4 53.3 %collective-permute-start.1 = (bf16[1,1,2,384,384]{3,4,2,1,0:T(8,128)(2,1)S(1)}, bf16[1,1,2,384,384]{3,4,2,1,0:T(8,128)(2,1)S(1)}, u32[]{:S(2)}, u32[]{:S(2)}) collective-permute-start(bf16[1,1,2,384,384]{3,4,2,1,0:T(8,128)(2,1)S(1)} %copy.3), channel_id=1, source_target_pairs={{56,0},{64,8},{72,16},{80,24},{88,32},{96,40},{104,48},{112,56},{1... | collective-permute-start | bytes 1769480 | tf_op jit(solution)/shard_map/ppermute | solution.py:13
  60.8 11.2 %collective-permute-start.2 = (bf16[1,1,2,384,384]{3,4,2,1,0:T(8,128)(2,1)S(1)}, bf16[1,1,2,384,384]{3,4,2,1,0:T(8,128)(2,1)S(1)}, u32[]{:S(2)}, u32[]{:S(2)}) collective-permute-start(bf16[1,1,2,384,384]{3,4,2,1,0:T(8,128)(2,1)S(1)} %add_convert_fusion.1), channel_id=1, source_target_pairs={{0,1},{1,2},{2,3},{3,4},{4,5},{5,6},{6,7},{8,9},{9,10},{10,11},{11... | collective-permute-start | bytes 1769480 | tf_op jit(solution)/shard_map/ppermute | solution.py:21
  62.8 12.4 %collective-permute-start.3 = (bf16[1,1,2,384,384]{3,4,2,1,0:T(8,128)(2,1)S(1)}, bf16[1,1,2,384,384]{3,4,2,1,0:T(8,128)(2,1)}, u32[]{:S(2)}, u32[]{:S(2)}) collective-permute-start(bf16[1,1,2,384,384]{3,4,2,1,0:T(8,128)(2,1)S(1)} %add_convert_fusion.1), channel_id=1, source_target_pairs={{1,0},{2,1},{3,2},{4,3},{5,4},{6,5},{7,6},{9,8},{10,9},{11,10},{12... | collective-permute-start | bytes 1769480 | tf_op jit(solution)/shard_map/ppermute | solution.py:24
  75.1 2.6 %copy-start = (bf16[1,1,2,384,384]{4,3,2,1,0:T(8,128)(2,1)S(1)}, bf16[1,1,2,384,384]{4,3,2,1,0:T(8,128)(2,1)}, u32[]{:S(2)}) copy-start(bf16[1,1,2,384,384]{4,3,2,1,0:T(8,128)(2,1)} %param.2) | copy-start | bytes 1769476
  81.2 49.9 %collective-permute-start.4 = (bf16[1,1,2,384,384]{4,3,2,1,0:T(8,128)(2,1)S(1)}, bf16[1,1,2,384,384]{4,3,2,1,0:T(8,128)(2,1)S(1)}, u32[]{:S(2)}, u32[]{:S(2)}) collective-permute-start(bf16[1,1,2,384,384]{4,3,2,1,0:T(8,128)(2,1)S(1)} %fusion.20), channel_id=1, source_target_pairs={{0,56},{8,64},{16,72},{24,80},{32,88},{40,96},{48,104},{56,112},{6... | collective-permute-start | bytes 1769480 | tf_op jit(solution)/shard_map/ppermute | solution.py:13
  111.4 33.0 %collective-permute-start.5 = (bf16[1,1,2,384,384]{4,3,2,1,0:T(8,128)(2,1)S(1)}, bf16[1,1,2,384,384]{4,3,2,1,0:T(8,128)(2,1)S(1)}, u32[]{:S(2)}, u32[]{:S(2)}) collective-permute-start(bf16[1,1,2,384,384]{4,3,2,1,0:T(8,128)(2,1)S(1)} %fusion.20), channel_id=1, source_target_pairs={{56,0},{64,8},{72,16},{80,24},{88,32},{96,40},{104,48},{112,56},{1... | collective-permute-start | bytes 1769480 | tf_op jit(solution)/shard_map/ppermute | solution.py:13
  144.6 11.3 %collective-permute-start.6 = (bf16[1,1,2,384,384]{4,3,2,1,0:T(8,128)(2,1)S(1)}, bf16[1,1,2,384,384]{4,3,2,1,0:T(8,128)(2,1)}, u32[]{:S(2)}, u32[]{:S(2)}) collective-permute-start(bf16[1,1,2,384,384]{4,3,2,1,0:T(8,128)(2,1)S(1)} %add_convert_fusion), channel_id=1, source_target_pairs={{0,1},{1,2},{2,3},{3,4},{4,5},{5,6},{6,7},{8,9},{9,10},{10,11},{11... | collective-permute-start | bytes 1769480 | tf_op jit(solution)/shard_map/ppermute | solution.py:21
  146.5 13.6 %collective-permute-start.7 = (bf16[1,1,2,384,384]{4,3,2,1,0:T(8,128)(2,1)S(1)}, bf16[1,1,2,384,384]{4,3,2,1,0:T(8,128)(2,1)}, u32[]{:S(2)}, u32[]{:S(2)}) collective-permute-start(bf16[1,1,2,384,384]{4,3,2,1,0:T(8,128)(2,1)S(1)} %add_convert_fusion), channel_id=1, source_target_pairs={{1,0},{2,1},{3,2},{4,3},{5,4},{6,5},{7,6},{9,8},{10,9},{11,10},{12... | collective-permute-start | bytes 1769480 | tf_op jit(solution)/shard_map/ppermute | solution.py:24
where the time goes:
time: 167 us
  waiting for transfers between devices  93.6 us (56%)
  starting transfers between devices  51.3 us (31%)
  matrix products  18.8 us (11%)
    ppermute x4, waiting for transfers between devices, passed_along(): lax.ppermute(value, axis, [(source, source + steps) for source in range(f...  82.4 us
    ppermute x4, starting transfers between devices, passed_along(): lax.ppermute(value, axis, [(source, source + steps) for source in range(f...  40 us
    dot_general x6, matrix products, dyson(): jnp.einsum('escij,skj->escik', left, weights, preferred_element_type=jnp....  12.4 us
    ppermute x2, waiting for transfers between devices, with_halo(): lax.ppermute(lax.slice_in_dim(block, block.shape[dim] - width, None, axis...  11.2 us
    ppermute x2, starting transfers between devices, with_halo(): lax.ppermute(lax.slice_in_dim(block, 0, width, axis=dim), axis, backward)  7.47 us
    ppermute x2, starting transfers between devices, with_halo(): lax.ppermute(lax.slice_in_dim(block, block.shape[dim] - width, None, axis...  3.84 us
  transfers between devices with their start and end apart: 8, of which 6 were waited for; matrix products, arithmetic and copies ran while one was open for 4% of the time, Pallas kernels for 0%

commit v1 on v0

v1 whole, which is shorter than its diff:
```python
import functools

import jax
import jax.numpy as jnp
from jax import lax
from jax.experimental import pallas as pl
from jax.experimental.pallas import tpu as pltpu
from jax.sharding import PartitionSpec as P

MESH = pl.DeviceIdType.MESH
B = 384
N = 3
R = B // N
BF = jnp.bfloat16
F32 = jnp.float32
NT = (((1,), (1,)), ((), ()))
SWAP, LOW, HIGH, WRAP, SIDE, HALO, VLOW, VHIGH, HALO2 = 0, 1, 2, 3, 4, 5, 9, 10, 11
KINDS = 13


def dot(a, b):
    return jnp.dot(a, b, preferred_element_type=F32)


def dot_nt(a, b):
    return lax.dot_general(a, b, NT, preferred_element_type=F32)


def kernel(
    g_in, c_in, out,
    base, recv, both, green, vrecv, both2, coup, ccat, rights, acc, sig, wide, outbuf,
    send_sem, recv_sem, local_sem,
):
    energy = lax.axis_index("energy")
    s = lax.axis_index("slab")
    g, z = energy // 8, energy % 8
    odd = g % 2
    mirror = g + 1 - 2 * odd
    lower_pair = g - 2 * (1 - odd)
    upper_pair = g + 2 * odd
    first, last = z == 0, z == 7
    edge = first | last
    inner = (z > 0) & (z < 7)
    zu, zd = (z + 1) % 8, (z + 7) % 8
    rows = [pl.ds(c * R, R) for c in range(N)]

    def at(gg, zz):
        return (gg * 8 + zz, s)

    home = (energy, s)
    up = (at(jnp.where(last, g, lower_pair), zu), last | (g >= 1))
    down = (at(jnp.where(first, g, upper_pair), zd), first | (g <= 6))
    vup = (at(jnp.where(last, g, mirror - 1), zu), last | (g != 1))
    vdown = (at(jnp.where(first, g, mirror + 1), zd), first | (g != 6))
    low_from = (at(jnp.where(first, g, mirror + 1), zd), first | (g != 6))
    high_from = (at(jnp.where(last, g, mirror - 1), zu), last | (g != 1))
    vlow_from = (at(jnp.where(first, g, upper_pair), zd), first | (g <= 6))
    vhigh_from = (at(jnp.where(last, g, lower_pair), zu), last | (g >= 1))
    slab_low, slab_high = (energy, s - 1), (energy, s + 1)
    side_in = (first & (g >= 1)) | (last & (g <= 6))
    side_out = ((z == 1) & (g != 6)) | ((z == 6) & (g != 1))

    def remote(kind, c, src, dst, dev):
        return pltpu.make_async_remote_copy(
            src_ref=src.at[rows[c]], dst_ref=dst.at[rows[c]],
            send_sem=send_sem.at[kind, c], recv_sem=recv_sem.at[kind, c],
            device_id=dev, device_id_type=MESH,
        )

    def start(kind, c, src, dst, dev, cond):
        @pl.when(cond)
        def _():
            remote(kind, c, src, dst, dev).start()

    def arrived(kind, c, dst, cond):
        @pl.when(cond)
        def _():
            remote(kind, c, dst, dst, home).wait_recv()

    def sent(kind, c, src, cond):
        @pl.when(cond)
        def _():
            remote(kind, c, src, src, home).wait_send()

    true = s >= 0
    mir, own = base.at[0], base.at[1]

    loads = [
        pltpu.make_async_copy(g_in.at[0], base.at[1, :, pl.ds(0, B)], local_sem.at[0]),
        pltpu.make_async_copy(g_in.at[1], base.at[1, :, pl.ds(B, B)], local_sem.at[1]),
        pltpu.make_async_copy(c_in, coup, local_sem.at[2]),
    ]
    for load in loads:
        load.start()

    barrier = pltpu.get_barrier_semaphore()
    pl.semaphore_signal(barrier, inc=1, device_id=at(mirror, z), device_id_type=MESH)
    count = jnp.int32(1)
    for dev, cond in (low_from, high_from, vlow_from, vhigh_from, (slab_low, s >= 1), (slab_high, s <= 6)):
        @pl.when(cond)
        def _(dev=dev):
            pl.semaphore_signal(barrier, inc=1, device_id=dev, device_id_type=MESH)
    for cond in (up[1], down[1], vup[1], vdown[1], s >= 1, s <= 6):
        count = count + cond.astype(jnp.int32)
    loads[0].wait()
    loads[1].wait()
    pl.semaphore_wait(barrier, count)

    for c in range(N):
        start(SWAP, c, own, mir, at(mirror, z), true)
        start(LOW, c, own, recv.at[0], *up)
        start(HIGH, c, own, recv.at[1], *down)

    def clear(ref, cond):
        @pl.when(cond)
        def _():
            ref[...] = jnp.zeros(ref.shape, ref.dtype)

    clear(recv.at[0], ~low_from[1])
    clear(recv.at[1], ~high_from[1])
    clear(recv.at[3], edge & ~side_in)
    clear(vrecv.at[0], ~vlow_from[1])
    clear(vrecv.at[1], ~vhigh_from[1])
    for target in (both.at[0], both.at[1], both2):
        clear(target.at[0], s == 0)
        clear(target.at[2], s == 7)

    loads[2].wait()
    for c in range(N):
        for k in range(3):
            ccat[c, :, k * R : (k + 1) * R] = coup[k, :, c * R : (c + 1) * R]

    def widen(j, c):
        re = base[j, rows[c], 0:B]
        im = base[j, rows[c], B : 2 * B]
        wide[j, pl.ds(c * R, R), 0:B] = re
        wide[j, pl.ds(c * R, R), B : 2 * B] = -im
        wide[j, pl.ds(B + c * R, R), 0:B] = im
        wide[j, pl.ds(B + c * R, R), B : 2 * B] = re

    for c in range(N):
        widen(1, c)

    def add_up(target, a, b, c):
        target[1, rows[c]] = (a[rows[c]].astype(F32) + b[rows[c]].astype(F32)).astype(BF)

    def pass_halo(kind, c, target):
        start(kind, c, target.at[1], target.at[2], slab_low, s >= 1)
        start(kind + 1, c, target.at[1], target.at[0], slab_high, s <= 6)

    def await_halo(kind, c, target, cond):
        arrived(kind, c, target.at[2], cond & (s <= 6))
        arrived(kind + 1, c, target.at[0], cond & (s >= 1))

    def sigma_part(target, c, to):
        for k in range(3):
            stacked = jnp.concatenate([target[k, rows[c], 0:B], target[k, rows[c], B : 2 * B]], axis=0)
            right = dot_nt(stacked, coup[k]).astype(BF)
            rights[k * R : (k + 1) * R, 0:B] = right[0:R]
            rights[k * R : (k + 1) * R, B : 2 * B] = right[R : 2 * R]
        part = dot(ccat[c], rights[...])
        if c == 0:
            to[...] = part
        else:
            to[...] += part

    def round_sigma(total):
        re = total[:, 0:B].astype(BF)
        im = total[:, B : 2 * B].astype(BF)
        sig[0:B, 0:B] = re
        sig[0:B, B : 2 * B] = im
        sig[B : 2 * B, 0:B] = -im
        sig[B : 2 * B, B : 2 * B] = re

    def result(j, c):
        here = base[j, rows[c]]
        prod = dot(here, sig[...]).astype(BF)
        return here.astype(F32) + dot_nt(prod, wide[j]) * (1.0 / B)

    for c in range(N):
        @pl.when(inner)
        def _(c=c):
            arrived(LOW, c, recv.at[0], low_from[1])
            arrived(HIGH, c, recv.at[1], high_from[1])
            add_up(both.at[0], recv.at[0], recv.at[1], c)
            pass_halo(HALO, c, both.at[0])

    for c in range(N):
        arrived(SWAP, c, mir, true)
        start(WRAP, c, mir, recv.at[2], at(g, jnp.where(first, 7, 0)), edge)
        start(SIDE, c, mir, recv.at[3],
              at(jnp.where(z == 1, mirror + 1, mirror - 1), jnp.where(z == 1, 0, 7)), side_out)
        widen(0, c)

        @pl.when(inner)
        def _(c=c):
            await_halo(HALO, c, both.at[0], true)
            sigma_part(both.at[0], c, acc.at[0])

    @pl.when(edge)
    def _():
        a0, b0 = jnp.where(first, 2, 0), jnp.where(last, 2, 1)
        a1, b1 = jnp.where(first, 0, 3), jnp.where(first, 3, 1)
        for c in range(N):
            arrived(LOW, c, recv.at[0], low_from[1])
            arrived(HIGH, c, recv.at[1], high_from[1])
            arrived(WRAP, c, recv.at[2], true)
            add_up(both.at[0], recv.at[a0], recv.at[b0], c)
            pass_halo(HALO, c, both.at[0])
            arrived(SIDE, c, recv.at[3], side_in)
            add_up(both.at[1], recv.at[a1], recv.at[b1], c)
            pass_halo(HALO + 2, c, both.at[1])
        for c in range(N):
            for j in range(2):
                await_halo(HALO + 2 * j, c, both.at[j], true)
                sigma_part(both.at[j], c, acc.at[j])

    round_sigma(acc.at[0])
    for c in range(N):
        green[0, rows[c]] = result(0, c).astype(BF)
        start(VLOW, c, green.at[0], vrecv.at[0], vup[0], vup[1] & ~last)
        start(VHIGH, c, green.at[0], vrecv.at[1], vdown[0], vdown[1] & ~first)

    @pl.when(edge)
    def _():
        round_sigma(acc.at[1])
        for c in range(N):
            green[1, rows[c]] = result(1, c).astype(BF)
            start(VLOW, c, green.at[1], vrecv.at[0], vup[0], last)
            start(VHIGH, c, green.at[1], vrecv.at[1], vdown[0], first)

    for c in range(N + 1):
        if c < N:
            arrived(VLOW, c, vrecv.at[0], vlow_from[1])
            arrived(VHIGH, c, vrecv.at[1], vhigh_from[1])
            add_up(both2, vrecv.at[0], vrecv.at[1], c)
            pass_halo(HALO2, c, both2)
        if c > 0:
            await_halo(HALO2, c - 1, both2, true)
            sigma_part(both2, c - 1, acc.at[0])
    round_sigma(acc.at[0])
    stores = []
    for c in range(N):
        outbuf[rows[c]] = result(1, c).astype(BF)
        for part in range(2):
            store = pltpu.make_async_copy(
                outbuf.at[rows[c], pl.ds(part * B, B)], out.at[part, rows[c]], local_sem.at[3 + 2 * c + part]
            )
            store.start()
            stores.append(store)

    for c in range(N):
        sent(SWAP, c, own, true)
        sent(LOW, c, own, up[1])
        sent(HIGH, c, own, down[1])
        sent(WRAP, c, mir, edge)
        sent(SIDE, c, mir, side_out)
        for j in range(2):
            cond = true if j == 0 else edge
            sent(HALO + 2 * j, c, both.at[j, 1], cond & (s >= 1))
            sent(HALO + 2 * j + 1, c, both.at[j, 1], cond & (s <= 6))
        sent(VLOW, c, green.at[0], vup[1])
        sent(VHIGH, c, green.at[0], vdown[1])
        sent(HALO2, c, both2.at[1], s >= 1)
        sent(HALO2 + 1, c, both2.at[1], s <= 6)
    for store in stores:
        store.wait()


def local(green0, coupling):
    block = (B, 2 * B)
    result = pl.pallas_call(
        kernel,
        out_shape=jax.ShapeDtypeStruct((2, B, B), BF),
        in_specs=[pl.BlockSpec(memory_space=pl.ANY)] * 2,
        out_specs=pl.BlockSpec(memory_space=pl.ANY),
        scratch_shapes=[
            pltpu.VMEM((2, *block), BF),
            pltpu.VMEM((4, *block), BF),
            pltpu.VMEM((2, 3, *block), BF),
            pltpu.VMEM((2, *block), BF),
            pltpu.VMEM((2, *block), BF),
            pltpu.VMEM((3, *block), BF),
            pltpu.VMEM((3, B, B), BF),
            pltpu.VMEM((N, B, 3 * R), BF),
            pltpu.VMEM((3 * R, 2 * B), BF),
            pltpu.VMEM((2, *block), F32),
            pltpu.VMEM((2 * B, 2 * B), BF),
            pltpu.VMEM((2, 2 * B, 2 * B), BF),
            pltpu.VMEM(block, BF),
            pltpu.SemaphoreType.DMA((KINDS, N)),
            pltpu.SemaphoreType.DMA((KINDS, N)),
            pltpu.SemaphoreType.DMA((3 + 2 * N,)),
        ],
        compiler_params=pltpu.CompilerParams(
            collective_id=0, has_side_effects=True, vmem_limit_bytes=48 * 1024 * 1024
        ),
        name="born",
    )(green0[0, 0], coupling[0])
    return result[None, None]


def solution(mesh):
    return jax.shard_map(
        local,
        mesh=mesh,
        in_specs=(P("energy", "slab", None, None, None), P("slab", None, None, None)),
        out_specs=P("energy", "slab", None, None, None),
        check_vma=False,
    )
```

time: 167 us -> 91.9 us (0.55)
  the two profiles are of different devices: /device:TPU:468 before, /device:TPU:1 now
where the time goes in v1:
time: 91.9 us; the launch traced here: 91.7 us
  Pallas kernels  88.6 us (96%)
  local copies, waits for them, and re-layouts  3.05 us (3%)
    pallas_call x1, Pallas kernels, local(): pl.pallas_call(kernel, out_shape=jax.ShapeDtypeStruct((2, B, B), BF), in_...  88.6 us
    unnamed x5, local copies, waits for them, and re-layouts  3.05 us

profile of v1, /device:TPU:1, one launch (start us, length us, event | category | flops | bytes accessed | tf_op | source)
XLA Modules:
  0.0 91.7 jit_solution(14734129314193312732)
XLA Ops:
  0.0 0.0 copy-start
  0.0 1.2 %copy-done = bf16[1,3,384,384]{3,2,1,0:T(8,128)(2,1)S(1)} copy-done((bf16[1,3,384,384]{3,2,1,0:T(8,128)(2,1)S(1)}, bf16[1,3,384,384]{3,2,1,0:T(8,128)(2,1)}, u32[]{:S(2)}) %copy-start) | copy-done | bytes 884760
  1.2 0.0 copy-start.1
  1.2 1.1 %copy-done.1 = bf16[1,1,2,384,384]{4,3,2,1,0:T(8,128)(2,1)S(1)} copy-done((bf16[1,1,2,384,384]{4,3,2,1,0:T(8,128)(2,1)S(1)}, bf16[1,1,2,384,384]{4,3,2,1,0:T(8,128)(2,1)}, u32[]{:S(2)}) %copy-start.1) | copy-done | bytes 589848
  2.2 88.6 %born.1 = bf16[2,384,384]{2,1,0:T(8,128)(2,1)S(1)} custom-call(bf16[2,384,384]{2,1,0:T(8,128)(2,1)S(1)} %bitcast.5, bf16[3,384,384]{2,1,0:T(8,128)(2,1)S(1)} %bitcast.4), custom_call_target="tpu_custom_call" | custom-call | tf_op jit(solution)/shard_map/born/pallas_call | solution.py:272
  90.8 0.8 copy.4
Async XLA Ops:
  0.0 1.2 %copy-start = (bf16[1,3,384,384]{3,2,1,0:T(8,128)(2,1)S(1)}, bf16[1,3,384,384]{3,2,1,0:T(8,128)(2,1)}, u32[]{:S(2)}) copy-start(bf16[1,3,384,384]{3,2,1,0:T(8,128)(2,1)} %param.3) | copy-start | bytes 2654212
  1.2 1.1 %copy-start.1 = (bf16[1,1,2,384,384]{4,3,2,1,0:T(8,128)(2,1)S(1)}, bf16[1,1,2,384,384]{4,3,2,1,0:T(8,128)(2,1)}, u32[]{:S(2)}) copy-start(bf16[1,1,2,384,384]{4,3,2,1,0:T(8,128)(2,1)} %param.2) | copy-start | bytes 1769476

commit v2 on v1

v2 whole, which is shorter than its diff:
```python
import functools

import jax
import jax.numpy as jnp
from jax import lax
from jax.experimental import pallas as pl
from jax.experimental.pallas import tpu as pltpu
from jax.sharding import PartitionSpec as P

MESH = pl.DeviceIdType.MESH
B = 384
N = 6
R = B // N
NC = 3
RC = B // NC
PER = N // NC
WINDOW = 3
NL = 3
LAG, LAG1, LAG2 = 2, 1, 2
BF = jnp.bfloat16
F32 = jnp.float32
NT = (((1,), (1,)), ((), ()))
SWAP, LOW, HIGH, WRAP, SIDE, HALO, VLOW, VHIGH, HALO2 = 0, 1, 2, 3, 4, 5, 9, 10, 11
RELAY, ONWARD = 13, 14
KINDS = 15
DETOURS = ((0, 4, 2), (0, 5, 3), (1, 5, 2))


def dot(a, b):
    return jnp.dot(a, b, preferred_element_type=F32)


def dot_nt(a, b):
    return lax.dot_general(a, b, NT, preferred_element_type=F32)


def kernel(
    g_in, c_in, out,
    base, recv, passing, both, green, vrecv, both2, coup, ccat, rights, acc, sig, wide,
    send_sem, recv_sem, local_sem,
):
    energy = lax.axis_index("energy")
    s = lax.axis_index("slab")
    g, z = energy // 8, energy % 8
    odd = g % 2
    mirror = g + 1 - 2 * odd
    lower_pair = g - 2 * (1 - odd)
    upper_pair = g + 2 * odd
    first, last = z == 0, z == 7
    edge = first | last
    zu, zd = (z + 1) % 8, (z + 7) % 8
    rows = [pl.ds(c * R, R) for c in range(N)]
    thick = [pl.ds(c * (B // NL), B // NL) for c in range(NL)]

    def piece(kind, c):
        return thick[c] if kind in (LOW, HIGH) else rows[c]

    def at(gg, zz):
        return (gg * 8 + zz, s)

    home = (energy, s)
    true = s >= 0
    up = (at(jnp.where(last, g, lower_pair), zu), last | (g >= 1))
    down = (at(jnp.where(first, g, upper_pair), zd), first | (g <= 6))
    vup = (at(jnp.where(last, g, mirror - 1), zu), last | (g != 1))
    vdown = (at(jnp.where(first, g, mirror + 1), zd), first | (g != 6))
    side_out = ((z == 1) & (g != 6)) | ((z == 6) & (g != 1))
    across = at(mirror, z)
    side_to = at(jnp.where(z == 1, mirror + 1, mirror - 1), jnp.where(z == 1, 0, 7))
    opposite = at(g, jnp.where(first, 7, 0))
    low_from = (at(jnp.where(first, g, mirror + 1), zd), first | (g != 6))
    high_from = (at(jnp.where(last, g, mirror - 1), zu), last | (g != 1))
    vlow_from = (at(jnp.where(first, g, upper_pair), zd), first | (g <= 6))
    vhigh_from = (at(jnp.where(last, g, lower_pair), zu), last | (g >= 1))
    slab_low, slab_high = ((energy, s - 1), s >= 1), ((energy, s + 1), s <= 6)
    side_in = (first & (g >= 1)) | (last & (g <= 6))

    def remote(kind, c, src, dst, dev, arrives):
        return pltpu.make_async_remote_copy(
            src_ref=src.at[piece(kind, c)], dst_ref=dst.at[piece(kind, c)],
            send_sem=send_sem.at[kind, c], recv_sem=recv_sem.at[arrives, c],
            device_id=dev, device_id_type=MESH,
        )

    def start(kind, c, src, dst, dev, cond, arrives=None):
        @pl.when(cond)
        def _():
            remote(kind, c, src, dst, dev, kind if arrives is None else arrives).start()

    def arrived(kind, c, dst, cond):
        @pl.when(cond)
        def _():
            remote(kind, c, dst, dst, home, kind).wait_recv()

    def sent(kind, c, src, cond):
        @pl.when(cond)
        def _():
            remote(kind, c, src, src, home, kind).wait_send()

    mir, own = base.at[0], base.at[1]

    loads = [
        pltpu.make_async_copy(g_in.at[0], base.at[1, :, pl.ds(0, B)], local_sem.at[0]),
        pltpu.make_async_copy(g_in.at[1], base.at[1, :, pl.ds(B, B)], local_sem.at[1]),
        pltpu.make_async_copy(c_in, coup, local_sem.at[2]),
    ]
    for load in loads:
        load.start()

    def flipped(zz):
        return jnp.where(z < 4, zz, 7 - zz)

    barrier = pltpu.get_barrier_semaphore()
    count = jnp.int32(1)
    for dev, cond in (
        low_from, high_from, vlow_from, vhigh_from, slab_low, slab_high,
        (across, true),
        *((at(g, flipped(source)), z == flipped(relay)) for source, _, relay in DETOURS),
        *((at(mirror, flipped(relay)), z == flipped(source)) for source, _, relay in DETOURS),
    ):
        @pl.when(cond)
        def _(dev=dev):
            pl.semaphore_signal(barrier, inc=1, device_id=dev, device_id_type=MESH)
    for cond in (
        up[1], down[1], vup[1], vdown[1], slab_low[1], slab_high[1],
        *(z == flipped(source) for source, _, _ in DETOURS),
        *(z == flipped(relay) for _, _, relay in DETOURS),
    ):
        count = count + cond.astype(jnp.int32)
    loads[0].wait()
    loads[1].wait()
    pl.semaphore_wait(barrier, count)

    def direct(c):
        cond = true
        for source, piece, _ in DETOURS:
            if piece == c:
                cond = cond & (z != flipped(source))
        return cond

    def detour(i):
        source, piece, relay = DETOURS[i]
        return pltpu.make_async_remote_copy(
            src_ref=own.at[rows[piece]], dst_ref=passing.at[i],
            send_sem=send_sem.at[RELAY, i], recv_sem=recv_sem.at[RELAY, i],
            device_id=at(g, flipped(relay)), device_id_type=MESH,
        )

    def onward(i):
        source, piece, relay = DETOURS[i]
        return pltpu.make_async_remote_copy(
            src_ref=passing.at[i], dst_ref=mir.at[rows[piece]],
            send_sem=send_sem.at[ONWARD, i], recv_sem=recv_sem.at[SWAP, piece],
            device_id=at(mirror, flipped(source)), device_id_type=MESH,
        )

    def swap(c):
        start(SWAP, c, own, mir, across, direct(c))

    for i, (source, _, _) in enumerate(DETOURS):
        @pl.when(z == flipped(source))
        def _(i=i):
            detour(i).start()
    for c in range(N):
        if c < WINDOW:
            swap(c)
        if c < NL:
            start(LOW, c, own, recv.at[0], *up)
            start(HIGH, c, own, recv.at[1], *down)

    def clear(ref, cond):
        @pl.when(cond)
        def _():
            ref[...] = jnp.zeros(ref.shape, ref.dtype)

    clear(recv.at[0], ~low_from[1])
    clear(recv.at[1], ~high_from[1])
    clear(recv.at[3], edge & ~side_in)
    clear(vrecv.at[0], ~vlow_from[1])
    clear(vrecv.at[1], ~vhigh_from[1])
    for target in (both.at[0], both.at[1], both2):
        clear(target.at[0], s == 0)
        clear(target.at[2], s == 7)

    loads[2].wait()
    for c in range(NC):
        for k in range(3):
            ccat[c, :, k * RC : (k + 1) * RC] = coup[k, :, c * RC : (c + 1) * RC]

    def widen(j, c):
        re = base[j, rows[c], 0:B]
        im = base[j, rows[c], B : 2 * B]
        wide[j, pl.ds(c * R, R), 0:B] = re
        wide[j, pl.ds(c * R, R), B : 2 * B] = -im
        wide[j, pl.ds(B + c * R, R), 0:B] = im
        wide[j, pl.ds(B + c * R, R), B : 2 * B] = re

    for c in range(N):
        widen(1, c)

    def add_up(target, a, b, c):
        target[1, rows[c]] = (a[rows[c]].astype(F32) + b[rows[c]].astype(F32)).astype(BF)

    def pass_halo(kind, c, target, cond=true):
        start(kind, c, target.at[1], target.at[2], slab_low[0], cond & slab_low[1])
        start(kind + 1, c, target.at[1], target.at[0], slab_high[0], cond & slab_high[1])

    def await_halo(kind, c, target):
        arrived(kind, c, target.at[2], slab_high[1])
        arrived(kind + 1, c, target.at[0], slab_low[1])

    def sigma_part(target, c, to):
        here = pl.ds(c * RC, RC)
        for k in range(3):
            stacked = jnp.concatenate([target[k, here, 0:B], target[k, here, B : 2 * B]], axis=0)
            right = dot_nt(stacked, coup[k]).astype(BF)
            rights[k * RC : (k + 1) * RC, 0:B] = right[0:RC]
            rights[k * RC : (k + 1) * RC, B : 2 * B] = right[RC : 2 * RC]
        part = dot(ccat[c], rights[...])
        if c == 0:
            to[...] = part
        else:
            to[...] += part

    def round_sigma(j):
        re = acc[j, :, 0:B].astype(BF)
        im = acc[j, :, B : 2 * B].astype(BF)
        sig[j, 0:B, 0:B] = re
        sig[j, 0:B, B : 2 * B] = im
        sig[j, B : 2 * B, 0:B] = -im
        sig[j, B : 2 * B, B : 2 * B] = re

    def result(j, c):
        here = base[j, pl.ds(c * RC, RC)]
        prod = dot(here, sig[j]).astype(BF)
        return here.astype(F32) + dot_nt(prod, wide[j]) * (1.0 / B)

    def next_swap(c):
        if c + WINDOW < N:
            sent(SWAP, c, own, direct(c))
            swap(c + WINDOW)

    def forward(c):
        arrived(SWAP, c, mir, true)
        next_swap(c)

    for i, (_, _, relay) in enumerate(DETOURS):
        @pl.when(z == flipped(relay))
        def _(i=i):
            detour(i).wait_recv()
            onward(i).start()

    @pl.when(~edge)
    def _():
        for c in range(N + LAG):
            if c < N:
                if c % (N // NL) == 0:
                    arrived(LOW, c // (N // NL), recv.at[0], low_from[1])
                    arrived(HIGH, c // (N // NL), recv.at[1], high_from[1])
                add_up(both.at[0], recv.at[0], recv.at[1], c)
                pass_halo(HALO, c, both.at[0])
                forward(c)
                start(SIDE, c, mir, recv.at[3], side_to, side_out)
                widen(0, c)
            d = c - LAG
            if d >= 0:
                await_halo(HALO, d, both.at[0])
                if d % PER == PER - 1:
                    sigma_part(both.at[0], d // PER, acc.at[0])

    @pl.when(edge)
    def _():
        a0, b0 = jnp.where(first, 2, 0), jnp.where(last, 2, 1)
        a1, b1 = jnp.where(first, 0, 3), jnp.where(first, 3, 1)
        for c in range(N + LAG2):
            if c < N:
                forward(c)
                start(WRAP, c, mir, recv.at[2], opposite, true)
                widen(0, c)
            d = c - LAG1
            if 0 <= d < N:
                if d % (N // NL) == 0:
                    arrived(LOW, d // (N // NL), recv.at[0], low_from[1])
                    arrived(HIGH, d // (N // NL), recv.at[1], high_from[1])
                arrived(WRAP, d, recv.at[2], true)
                add_up(both.at[0], recv.at[a0], recv.at[b0], d)
                pass_halo(HALO, d, both.at[0])
                arrived(SIDE, d, recv.at[3], side_in)
                add_up(both.at[1], recv.at[a1], recv.at[b1], d)
                pass_halo(HALO + 2, d, both.at[1])
            d = c - LAG2
            if d >= 0:
                for j in range(2):
                    await_halo(HALO + 2 * j, d, both.at[j])
                    if d % PER == PER - 1:
                        sigma_part(both.at[j], d // PER, acc.at[j])
        round_sigma(1)

    round_sigma(0)
    for c in range(NC):
        @pl.when(edge)
        def _(c=c):
            green[1, pl.ds(c * RC, RC)] = result(1, c).astype(BF)
            for d in range(c * PER, c * PER + PER):
                start(VLOW, d, green.at[1], vrecv.at[0], vup[0], last)
                start(VHIGH, d, green.at[1], vrecv.at[1], vdown[0], first)
        green[0, pl.ds(c * RC, RC)] = result(0, c).astype(BF)
        for d in range(c * PER, c * PER + PER):
            start(VLOW, d, green.at[0], vrecv.at[0], vup[0], vup[1] & ~last)
            start(VHIGH, d, green.at[0], vrecv.at[1], vdown[0], vdown[1] & ~first)

    for c in range(N + PER):
        if c < N:
            arrived(VLOW, c, vrecv.at[0], vlow_from[1])
            arrived(VHIGH, c, vrecv.at[1], vhigh_from[1])
            add_up(both2, vrecv.at[0], vrecv.at[1], c)
            pass_halo(HALO2, c, both2)
        d = c - PER
        if d >= 0:
            await_halo(HALO2, d, both2)
            if d % PER == PER - 1:
                sigma_part(both2, d // PER, acc.at[1])
    round_sigma(1)
    for c in range(NC):
        here = pl.ds(c * RC, RC)
        final = result(1, c).astype(BF)
        for part in range(2):
            out[part, here] = final[:, part * B : part * B + B]

    for c in range(N):
        if c + WINDOW >= N:
            sent(SWAP, c, own, direct(c))
        if c < NL:
            sent(LOW, c, own, up[1])
            sent(HIGH, c, own, down[1])
        sent(WRAP, c, mir, edge)
        sent(SIDE, c, mir, side_out)
        for j in range(2):
            cond = true if j == 0 else edge
            sent(HALO + 2 * j, c, both.at[j, 1], cond & slab_low[1])
            sent(HALO + 2 * j + 1, c, both.at[j, 1], cond & slab_high[1])
        sent(VLOW, c, green.at[0], vup[1])
        sent(VHIGH, c, green.at[0], vdown[1])
        sent(HALO2, c, both2.at[1], slab_low[1])
        sent(HALO2 + 1, c, both2.at[1], slab_high[1])
    for i, (source, _, relay) in enumerate(DETOURS):
        @pl.when(z == flipped(source))
        def _(i=i):
            detour(i).wait_send()

        @pl.when(z == flipped(relay))
        def _(i=i):
            onward(i).wait_send()


def local(green0, coupling):
    block = (B, 2 * B)
    result = pl.pallas_call(
        kernel,
        out_shape=jax.ShapeDtypeStruct((2, B, B), BF),
        in_specs=[pl.BlockSpec(memory_space=pltpu.HBM)] * 2,
        out_specs=pl.BlockSpec(memory_space=pltpu.VMEM),
        scratch_shapes=[
            pltpu.VMEM((2, *block), BF),
            pltpu.VMEM((4, *block), BF),
            pltpu.VMEM((len(DETOURS), R, 2 * B), BF),
            pltpu.VMEM((2, 3, *block), BF),
            pltpu.VMEM((2, *block), BF),
            pltpu.VMEM((2, *block), BF),
            pltpu.VMEM((3, *block), BF),
            pltpu.VMEM((3, B, B), BF),
            pltpu.VMEM((NC, B, 3 * RC), BF),
            pltpu.VMEM((3 * RC, 2 * B), BF),
            pltpu.VMEM((2, *block), F32),
            pltpu.VMEM((2, 2 * B, 2 * B), BF),
            pltpu.VMEM((2, 2 * B, 2 * B), BF),
            pltpu.SemaphoreType.DMA((KINDS, N)),
            pltpu.SemaphoreType.DMA((KINDS, N)),
            pltpu.SemaphoreType.DMA((3,)),
        ],
        compiler_params=pltpu.CompilerParams(
            collective_id=0, has_side_effects=True, vmem_limit_bytes=53 * 1024 * 1024
        ),
        name="born",
    )(green0[0, 0], coupling[0])
    return result[None, None]


def solution(mesh):
    return jax.shard_map(
        local,
        mesh=mesh,
        in_specs=(P("energy", "slab", None, None, None), P("slab", None, None, None)),
        out_specs=P("energy", "slab", None, None, None),
        check_vma=False,
    )
```

time: 91.9 us -> 76.6 us (0.83)
  Pallas kernels: 88.6 us -> 75.6 us
  local copies, waits for them, and re-layouts: 3.05 us -> 0.82 us
    pallas_call x1, Pallas kernels: 88.6 us -> 75.6 us  [local(): pl.pallas_call(kernel, out_shape=jax.ShapeDtypeStruct((2, B, B), BF), in_...]
    unnamed x5 -> x1, local copies, waits for them, and re-layouts: 3.05 us -> 0.82 us
where the time goes in v2:
time: 76.6 us; the launch traced here: 76.5 us
  Pallas kernels  75.6 us (99%)
  local copies, waits for them, and re-layouts  0.82 us (1%)
    pallas_call x1, Pallas kernels, local(): pl.pallas_call(kernel, out_shape=jax.ShapeDtypeStruct((2, B, B), BF), in_...  75.6 us

profile of v2, /device:TPU:1, one launch (start us, length us, event | category | flops | bytes accessed | tf_op | source)
XLA Modules:
  0.0 76.5 jit_solution(3217097009339435632)
XLA Ops:
  0.0 75.6 %born.1 = bf16[2,384,384]{2,1,0:T(8,128)(2,1)S(1)} custom-call(bf16[2,384,384]{2,1,0:T(8,128)(2,1)} %bitcast.5, bf16[3,384,384]{2,1,0:T(8,128)(2,1)} %bitcast.4), custom_call_target="tpu_custom_call" | custom-call | tf_op jit(solution)/shard_map/born/pallas_call | solution.py:358
  75.6 0.8 %copy.4 = bf16[1,1,2,384,384]{4,3,2,1,0:T(8,128)(2,1)} copy(bf16[1,1,2,384,384]{4,3,2,1,0:T(8,128)(2,1)S(1)} %bitcast.3) | data formatting | bytes 1179648

commit v3 on v2

--- a/solution.py
+++ b/solution.py
@@ -16,7 +16,7 @@
 PER = N // NC
 WINDOW = 3
 NL = 3
-LAG, LAG1, LAG2 = 2, 1, 2
+LAG, LAG1, LAG2 = 2, 2, 3
 BF = jnp.bfloat16
 F32 = jnp.float32
 NT = (((1,), (1,)), ((), ()))
@@ -230,8 +230,8 @@
         sig[j, B : 2 * B, 0:B] = -im
         sig[j, B : 2 * B, B : 2 * B] = re
 
-    def result(j, c):
-        here = base[j, pl.ds(c * RC, RC)]
+    def result(j, lines):
+        here = base[j, lines]
         prod = dot(here, sig[j]).astype(BF)
         return here.astype(F32) + dot_nt(prod, wide[j]) * (1.0 / B)
 
@@ -300,11 +300,11 @@
     for c in range(NC):
         @pl.when(edge)
         def _(c=c):
-            green[1, pl.ds(c * RC, RC)] = result(1, c).astype(BF)
+            green[1, pl.ds(c * RC, RC)] = result(1, pl.ds(c * RC, RC)).astype(BF)
             for d in range(c * PER, c * PER + PER):
                 start(VLOW, d, green.at[1], vrecv.at[0], vup[0], last)
                 start(VHIGH, d, green.at[1], vrecv.at[1], vdown[0], first)
-        green[0, pl.ds(c * RC, RC)] = result(0, c).astype(BF)
+        green[0, pl.ds(c * RC, RC)] = result(0, pl.ds(c * RC, RC)).astype(BF)
         for d in range(c * PER, c * PER + PER):
             start(VLOW, d, green.at[0], vrecv.at[0], vup[0], vup[1] & ~last)
             start(VHIGH, d, green.at[0], vrecv.at[1], vdown[0], vdown[1] & ~first)
@@ -321,11 +321,9 @@
             if d % PER == PER - 1:
                 sigma_part(both2, d // PER, acc.at[1])
     round_sigma(1)
-    for c in range(NC):
-        here = pl.ds(c * RC, RC)
-        final = result(1, c).astype(BF)
-        for part in range(2):
-            out[part, here] = final[:, part * B : part * B + B]
+    final = result(1, slice(None)).astype(BF)
+    for part in range(2):
+        out[part] = final[:, part * B : part * B + B]
 
     for c in range(N):
         if c + WINDOW >= N:

time: 76.6 us -> 75.9 us (level)
  no operation moved by 1% of the time
where the time goes in v3:
time: 75.9 us; the launch traced here: 75.8 us
  Pallas kernels  75 us (99%)
  local copies, waits for them, and re-layouts  0.82 us (1%)
    pallas_call x1, Pallas kernels, local(): pl.pallas_call(kernel, out_shape=jax.ShapeDtypeStruct((2, B, B), BF), in_...  75 us

profile of v3, /device:TPU:1, one launch (start us, length us, event | category | flops | bytes accessed | tf_op | source)
XLA Modules:
  0.0 75.8 jit_solution(12545261987521542017)
XLA Ops:
  0.0 75.0 %born.1 = bf16[2,384,384]{2,1,0:T(8,128)(2,1)S(1)} custom-call(bf16[2,384,384]{2,1,0:T(8,128)(2,1)} %bitcast.5, bf16[3,384,384]{2,1,0:T(8,128)(2,1)} %bitcast.4), custom_call_target="tpu_custom_call" | custom-call | tf_op jit(solution)/shard_map/born/pallas_call | solution.py:356
  75.0 0.8 %copy.4 = bf16[1,1,2,384,384]{4,3,2,1,0:T(8,128)(2,1)} copy(bf16[1,1,2,384,384]{4,3,2,1,0:T(8,128)(2,1)S(1)} %bitcast.3) | data formatting | bytes 1179648
